TPU v7x, 32 devices: a whole 2x2x4 slice. The times are simulated.
32 devices in a mesh: ctx: 16 (over z, x, core), kvh: 2 (over y).
Axes of the slice: x: 2, y: 2, z: 4, core: 2. Of those that a mesh axis runs over, the one named last changes fastest.
Arguments:
- queries: bfloat16 [8192, 8192], P('ctx', 'kvh')
- key_vector_rows: bfloat16 [8192, 1024], P('ctx', 'kvh')
- value_vector_rows: bfloat16 [8192, 1024], P('ctx', 'kvh'), may hold values from -6 to 6
- block_picks: int32 [64, 8], P('ctx'), may hold values from 0 to 63, as said below
Outputs:
- attended: bfloat16 [8192, 8192], P(('ctx', 'kvh'))
Inputs may be any that keep to these rules, and one draw needn't show every extreme that they name: block_picks[b, 0] = b. The other entries of a row name 7 distinct blocks that lie on other indices of ctx (block c lies on index c // 4). Over the 4 rows of one index of ctx, the entries naming blocks of any one other index are at most 2 and name at most 1 distinct blocks; both bounds are reached in every draw.
All inputs are finite; a program needn't handle non-finite values.
Results may differ from a plain program's by a relative error of at most 0.0047.
Values may be sent and summed in bfloat16 or wider, within the bound.
A program may use at most 64 MiB of HBM per device.

v0:
```python
import math

import jax
import jax.numpy as jnp
from jax import lax
from jax.sharding import PartitionSpec as P

HEAD_SIZE = 128
BLOCK_TOKENS = 128
PICKED_BLOCKS = 8


def plan_distinct(remote, blocks, peer_count, capacity):
    flat_picks = remote.reshape(-1)
    owners = flat_picks // blocks
    local_ids = flat_picks % blocks
    owner_hits = (owners[:, None] == jnp.arange(peer_count, dtype=jnp.int32)[None, :]).astype(
        jnp.int32
    )
    local_hits = (local_ids[:, None] == jnp.arange(blocks, dtype=jnp.int32)[None, :]).astype(
        jnp.int32
    )
    needed = (jnp.dot(owner_hits.T, local_hits) > 0).astype(jnp.int32)
    places = jnp.cumsum(needed, axis=1) * needed - 1
    slot_rank = places[owners, local_ids]
    place_hits = (
        places[:, :, None] == jnp.arange(capacity, dtype=jnp.int32)[None, None, :]
    ).astype(jnp.int32)
    requests = jnp.sum(place_hits * jnp.arange(blocks, dtype=jnp.int32)[None, :, None], axis=1)
    return (requests, slot_rank)


def block_attention(query_block, kv_block, kv_heads):
    block_len = query_block.shape[0]
    pick_count = kv_block.shape[0]
    group_size = query_block.shape[1] // (kv_heads * HEAD_SIZE)
    query_heads = query_block.reshape(block_len, kv_heads, group_size, HEAD_SIZE)
    stacked = kv_block.reshape(pick_count * block_len, 2, kv_heads, HEAD_SIZE)
    key_selection = stacked[:, 0]
    value_selection = stacked[:, 1]
    scores = jnp.einsum(
        "qgxd,kgd->gxqk", query_heads, key_selection, preferred_element_type=jnp.float32
    )
    scores = scores * (1.0 / math.sqrt(HEAD_SIZE))
    positions = jnp.arange(block_len, dtype=jnp.int32)
    causal = positions[None, :] <= positions[:, None]
    visible = jnp.concatenate(
        [causal, jnp.ones((block_len, (pick_count - 1) * block_len), dtype=bool)], axis=1
    )
    scores = jnp.where(visible, scores, -jnp.inf)
    row_max = jnp.max(scores, axis=-1, keepdims=True)
    exponents = jnp.exp(scores - row_max)
    totals = jnp.sum(exponents, axis=-1, keepdims=True)
    weights = exponents.astype(jnp.bfloat16)
    blended = jnp.einsum(
        "gxqk,kgd->qgxd", weights, value_selection, preferred_element_type=jnp.float32
    )
    blended = blended / jnp.transpose(totals, (2, 0, 1, 3))
    return blended.reshape(block_len, -1).astype(jnp.bfloat16)


def body(queries, key_vector_rows, value_vector_rows, block_picks):
    peer_count = lax.axis_size("ctx")
    my_index = lax.axis_index("ctx")
    tok_dev = key_vector_rows.shape[0]
    blocks = tok_dev // BLOCK_TOKENS
    kv_heads = key_vector_rows.shape[1] // HEAD_SIZE
    local_kv = jnp.concatenate([key_vector_rows, value_vector_rows], axis=1).reshape(
        blocks, BLOCK_TOKENS, 2 * kv_heads * HEAD_SIZE
    )
    remote = block_picks[:, 1:]
    far_count = blocks * (PICKED_BLOCKS - 1)
    distinct_cap = (far_count // 2 + peer_count - 2) // (peer_count - 1)
    requests, slot_rank = plan_distinct(remote, blocks, peer_count, distinct_cap)
    pick_table = lax.all_gather(block_picks, "ctx", axis=0, tiled=True)
    all_rows = pick_table[:, 1:].reshape(peer_count, blocks, PICKED_BLOCKS - 1)

    def requests_of(rows_one):
        return plan_distinct(rows_one, blocks, peer_count, distinct_cap)[0]

    all_requests = jax.vmap(requests_of)(all_rows)
    wanted = jnp.take(all_requests, my_index, axis=1)
    outgoing = local_kv[wanted]
    incoming = lax.all_to_all(outgoing, "ctx", split_axis=0, concat_axis=0, tiled=True)
    owners = (remote // blocks).reshape(-1)
    fetched = incoming.reshape(peer_count * distinct_cap, BLOCK_TOKENS, -1)[
        owners * distinct_cap + slot_rank
    ]
    fetched = fetched.reshape(blocks, PICKED_BLOCKS - 1, BLOCK_TOKENS, -1)
    chosen = jnp.concatenate([local_kv[:, None], fetched], axis=1)

    def attend_pair(pair):
        return block_attention(pair[0], pair[1], kv_heads)

    attended = lax.map(attend_pair, (queries.reshape(blocks, BLOCK_TOKENS, -1), chosen))
    attended = attended.reshape(tok_dev, -1)
    return lax.all_to_all(attended, "kvh", split_axis=0, concat_axis=1, tiled=True)


def solution(mesh):
    return jax.shard_map(
        body,
        mesh=mesh,
        in_specs=(P("ctx", "kvh"), P("ctx", "kvh"), P("ctx", "kvh"), P("ctx", None)),
        out_specs=P(("ctx", "kvh"), None),
        check_vma=False,
    )
```

profile of v0, /device:TPU:10, one launch (start us, length us, event | category | flops | bytes accessed | tf_op | source)
XLA Modules:
  0.0 374.0 jit_solution(2695168310409646764)
XLA Ops:
  0.0 15.4 %all-gather = s32[16,4,8]{2,1,0:T(4,128)S(1)} all-gather(s32[1,4,8]{2,1,0:T(4,128)} %bitcast.97), channel_id=1, replica_groups=mesh['ctx'=16,'kvh'=2] {'ctx'}, dimensions={0}, use_global_device_ids=true | all-gather | bytes 2176 | tf_op jit(solution)/shard_map/all_gather | solution.py:75
  21.1 11.2 %all-to-all-start = ((bf16[16,1,128,1024]{3,2,1,0:T(8,128)(2,1)}), bf16[16,1,128,1024]{3,2,1,0:T(8,128)(2,1)}, u32[]{:S(2)}, u32[]{:S(2)}) async-start(bf16[16,1,128,1024]{3,2,1,0:T(8,128)(2,1)} %bitcast.90), calls=%async_computation | async-start | bytes 8388608 | tf_op jit(solution)/shard_map/all_to_all | solution.py:84
  33.8 90.8 %all-to-all-done = bf16[16,1,128,1024]{3,2,1,0:T(8,128)(2,1)} async-done(((bf16[16,1,128,1024]{3,2,1,0:T(8,128)(2,1)}), bf16[16,1,128,1024]{3,2,1,0:T(8,128)(2,1)}, u32[]{:S(2)}, u32[]{:S(2)}) %all-to-all-start) | async-done | bytes 4194336 | tf_op jit(solution)/shard_map/all_to_all | solution.py:84
  124.6 7.0 %gather_fusion.2 = bf16[28,128,1024]{2,1,0:T(8,128)(2,1)} fusion(bf16[16,128,1024]{2,1,0:T(8,128)(2,1)} %bitcast.20, s32[1024]{0:T(1024)S(1)} %pad_clamp_fusion), kind=kCustom, calls=%fused_computation.2 | custom fusion | bytes 14680176 | tf_op jit(solution)/shard_map/gather | solution.py:86
  131.6 7.0 %pad_maximum_fusion = bf16[4,8,128,1024]{3,2,1,0:T(8,128)(2,1)} fusion(bf16[4,7,128,1024]{3,2,1,0:T(8,128)(2,1)} %bitcast.88, bf16[4,1,128,1024]{3,2,1,0:T(8,128)(2,1)S(1)} %bitcast.87), kind=kLoop, calls=%fused_computation.21 | loop fusion | flops 4194304 | bytes 16777216 | tf_op jit(solution)/shard_map/concatenate | solution.py:90
  138.6 167.2 %while.11 = (s32[]{:T(128)}, bf16[4,128,4096]{2,1,0:T(8,128)(2,1)}, bf16[4,8,128,1024]{3,2,1,0:T(8,128)(2,1)}, bf16[4,128,4096]{2,1,0:T(8,128)(2,1)}, s32[]{:T(128)}, /*index=5*/pred[]{:T(512)}) while((s32[]{:T(128)}, bf16[4,128,4096]{2,1,0:T(8,128)(2,1)}, bf16[4,8,128,1024]{3,2,1,0:T(8,128)(2,1)}, bf16[4,128,4096]{2,1,0:T(8,128)(2,1)}, ...), condition=%wide.region_6.7_spmd, body=%wide.region_3.6_spmd.sunk | while | flops 2194677760 | bytes 80331336 | solution.py:95
  141.7 3.2 reshape.362
  151.0 8.3 %fusion.50 = (f32[4,8,128]{2,1,0:T(8,128)S(1)}, f32[4,1024,128,8]{2,1,3,0:T(8,128)}) fusion(pred[128,1024]{0,1:T(8,128)(4,1)S(1)} %concatenate.19, bf16[128,4,8,128]{0,3,2,1:T(8,128)(2,1)} %bitcast.85, bf16[1024,1,4,128]{0,3,2,1:T(8,128)(2,1)S(1)} %copy.56), kind=kOutput, calls=%fused_computation.7.clone.1 | convolution fusion | flops 1086320640 | bytes 19021824 | tf_op jit(solution)/shard_map/while/body/eval_jaxpr/qgxd,kgd->gxqk/dot_general | solution.py:41
  159.3 9.1 %fusion.51 = f32[4,8,128]{2,1,0:T(8,128)S(1)} fusion(f32[4,1024,128,8]{2,1,3,0:T(8,128)} %get-tuple-element.101, f32[4,8,128]{2,1,0:T(8,128)S(1)} %get-tuple-element.102, pred[128,1024]{0,1:T(8,128)(4,1)S(1)} %concatenate.19), kind=kLoop, calls=%fused_computation.5.clone.1 | loop fusion | flops 16773120 | bytes 16941056 | tf_op jit(solution)/shard_map/while/body/eval_jaxpr/reduce_sum | solution.py:53
  169.1 9.7 %fusion.52 = bf16[128,4,8,128]{0,3,2,1:T(8,128)(2,1)S(1)} fusion(f32[4,1024,128,8]{2,1,3,0:T(8,128)} %get-tuple-element.101, f32[4,8,128]{2,1,0:T(8,128)S(1)} %get-tuple-element.102, pred[128,1024]{0,1:T(8,128)(4,1)S(1)} %concatenate.19, bf16[1024,1,4,128]{0,3,2,1:T(8,128)(2,1)S(1)} %copy.57, f32[128,4,8]{0,2,1:T(8,128)S(1)} %bitcast.95), kind=kOutput, calls=%fused_computation.11.clone.1 | convolution fusion | flops 1091567616 | bytes 19038208 | tf_op jit(solution)/shard_map/while/body/eval_jaxpr/gxqk,kgd->qgxd/dot_general | solution.py:55
  183.5 3.2 reshape.362
  192.8 8.3 %fusion.50 = (f32[4,8,128]{2,1,0:T(8,128)S(1)}, f32[4,1024,128,8]{2,1,3,0:T(8,128)}) fusion(pred[128,1024]{0,1:T(8,128)(4,1)S(1)} %concatenate.19, bf16[128,4,8,128]{0,3,2,1:T(8,128)(2,1)} %bitcast.85, bf16[1024,1,4,128]{0,3,2,1:T(8,128)(2,1)S(1)} %copy.56), kind=kOutput, calls=%fused_computation.7.clone.1 | convolution fusion | flops 1086320640 | bytes 19021824 | tf_op jit(solution)/shard_map/while/body/eval_jaxpr/qgxd,kgd->gxqk/dot_general | solution.py:41
  201.1 9.1 %fusion.51 = f32[4,8,128]{2,1,0:T(8,128)S(1)} fusion(f32[4,1024,128,8]{2,1,3,0:T(8,128)} %get-tuple-element.101, f32[4,8,128]{2,1,0:T(8,128)S(1)} %get-tuple-element.102, pred[128,1024]{0,1:T(8,128)(4,1)S(1)} %concatenate.19), kind=kLoop, calls=%fused_computation.5.clone.1 | loop fusion | flops 16773120 | bytes 16941056 | tf_op jit(solution)/shard_map/while/body/eval_jaxpr/reduce_sum | solution.py:53
  210.9 9.7 %fusion.52 = bf16[128,4,8,128]{0,3,2,1:T(8,128)(2,1)S(1)} fusion(f32[4,1024,128,8]{2,1,3,0:T(8,128)} %get-tuple-element.101, f32[4,8,128]{2,1,0:T(8,128)S(1)} %get-tuple-element.102, pred[128,1024]{0,1:T(8,128)(4,1)S(1)} %concatenate.19, bf16[1024,1,4,128]{0,3,2,1:T(8,128)(2,1)S(1)} %copy.57, f32[128,4,8]{0,2,1:T(8,128)S(1)} %bitcast.95), kind=kOutput, calls=%fused_computation.11.clone.1 | convolution fusion | flops 1091567616 | bytes 19038208 | tf_op jit(solution)/shard_map/while/body/eval_jaxpr/gxqk,kgd->qgxd/dot_general | solution.py:55
  225.3 3.2 reshape.362
  234.6 8.3 %fusion.50 = (f32[4,8,128]{2,1,0:T(8,128)S(1)}, f32[4,1024,128,8]{2,1,3,0:T(8,128)}) fusion(pred[128,1024]{0,1:T(8,128)(4,1)S(1)} %concatenate.19, bf16[128,4,8,128]{0,3,2,1:T(8,128)(2,1)} %bitcast.85, bf16[1024,1,4,128]{0,3,2,1:T(8,128)(2,1)S(1)} %copy.56), kind=kOutput, calls=%fused_computation.7.clone.1 | convolution fusion | flops 1086320640 | bytes 19021824 | tf_op jit(solution)/shard_map/while/body/eval_jaxpr/qgxd,kgd->gxqk/dot_general | solution.py:41
  242.9 9.1 %fusion.51 = f32[4,8,128]{2,1,0:T(8,128)S(1)} fusion(f32[4,1024,128,8]{2,1,3,0:T(8,128)} %get-tuple-element.101, f32[4,8,128]{2,1,0:T(8,128)S(1)} %get-tuple-element.102, pred[128,1024]{0,1:T(8,128)(4,1)S(1)} %concatenate.19), kind=kLoop, calls=%fused_computation.5.clone.1 | loop fusion | flops 16773120 | bytes 16941056 | tf_op jit(solution)/shard_map/while/body/eval_jaxpr/reduce_sum | solution.py:53
  252.7 9.7 %fusion.52 = bf16[128,4,8,128]{0,3,2,1:T(8,128)(2,1)S(1)} fusion(f32[4,1024,128,8]{2,1,3,0:T(8,128)} %get-tuple-element.101, f32[4,8,128]{2,1,0:T(8,128)S(1)} %get-tuple-element.102, pred[128,1024]{0,1:T(8,128)(4,1)S(1)} %concatenate.19, bf16[1024,1,4,128]{0,3,2,1:T(8,128)(2,1)S(1)} %copy.57, f32[128,4,8]{0,2,1:T(8,128)S(1)} %bitcast.95), kind=kOutput, calls=%fused_computation.11.clone.1 | convolution fusion | flops 1091567616 | bytes 19038208 | tf_op jit(solution)/shard_map/while/body/eval_jaxpr/gxqk,kgd->qgxd/dot_general | solution.py:55
  276.4 8.3 %fusion.50 = (f32[4,8,128]{2,1,0:T(8,128)S(1)}, f32[4,1024,128,8]{2,1,3,0:T(8,128)}) fusion(pred[128,1024]{0,1:T(8,128)(4,1)S(1)} %concatenate.19, bf16[128,4,8,128]{0,3,2,1:T(8,128)(2,1)} %bitcast.85, bf16[1024,1,4,128]{0,3,2,1:T(8,128)(2,1)S(1)} %copy.56), kind=kOutput, calls=%fused_computation.7.clone.1 | convolution fusion | flops 1086320640 | bytes 19021824 | tf_op jit(solution)/shard_map/while/body/eval_jaxpr/qgxd,kgd->gxqk/dot_general | solution.py:41
  284.7 9.1 %fusion.51 = f32[4,8,128]{2,1,0:T(8,128)S(1)} fusion(f32[4,1024,128,8]{2,1,3,0:T(8,128)} %get-tuple-element.101, f32[4,8,128]{2,1,0:T(8,128)S(1)} %get-tuple-element.102, pred[128,1024]{0,1:T(8,128)(4,1)S(1)} %concatenate.19), kind=kLoop, calls=%fused_computation.5.clone.1 | loop fusion | flops 16773120 | bytes 16941056 | tf_op jit(solution)/shard_map/while/body/eval_jaxpr/reduce_sum | solution.py:53
  294.5 9.7 %fusion.52 = bf16[128,4,8,128]{0,3,2,1:T(8,128)(2,1)S(1)} fusion(f32[4,1024,128,8]{2,1,3,0:T(8,128)} %get-tuple-element.101, f32[4,8,128]{2,1,0:T(8,128)S(1)} %get-tuple-element.102, pred[128,1024]{0,1:T(8,128)(4,1)S(1)} %concatenate.19, bf16[1024,1,4,128]{0,3,2,1:T(8,128)(2,1)S(1)} %copy.57, f32[128,4,8]{0,2,1:T(8,128)S(1)} %bitcast.95), kind=kOutput, calls=%fused_computation.11.clone.1 | convolution fusion | flops 1091567616 | bytes 19038208 | tf_op jit(solution)/shard_map/while/body/eval_jaxpr/gxqk,kgd->qgxd/dot_general | solution.py:55
  305.8 55.5 %all_to_all.24 = bf16[2,256,4096]{2,1,0:T(8,128)(2,1)} all-to-all(bf16[2,256,4096]{2,1,0:T(8,128)(2,1)} %bitcast.94), channel_id=1, replica_groups=mesh['ctx'=16,'kvh'=2] {'kvh'}, dimensions={0} | all-to-all | bytes 8388608 | tf_op jit(solution)/shard_map/all_to_all | solution.py:97
  361.3 6.4 %copy.36 = bf16[256,2,4096]{0,2,1:T(8,128)(2,1)} copy(bf16[256,2,4096]{2,0,1:T(8,128)(2,1)} %bitcast.91) | data formatting | bytes 8388608 | tf_op jit(solution)/shard_map/all_to_all | solution.py:97
  367.7 6.3 %copy.37 = bf16[256,8192]{1,0:T(8,128)(2,1)} copy(bf16[256,8192]{0,1:T(8,128)(2,1)} %bitcast.92) | data formatting | bytes 8388608 | tf_op jit(solution)/shard_map/all_to_all | solution.py:97
  (69 shorter events, 56.0 us)
Async XLA Ops:
  18.3 14.0 %copy-start = (s32[4,8]{1,0:T(4,128)S(1)}, s32[4,8]{1,0:T(4,128)}, u32[]{:S(2)}) copy-start(s32[4,8]{1,0:T(4,128)} %param.9) | copy-start | bytes 388
  21.1 103.6 %all-to-all-start = ((bf16[16,1,128,1024]{3,2,1,0:T(8,128)(2,1)}), bf16[16,1,128,1024]{3,2,1,0:T(8,128)(2,1)}, u32[]{:S(2)}, u32[]{:S(2)}) async-start(bf16[16,1,128,1024]{3,2,1,0:T(8,128)(2,1)} %bitcast.90), calls=%async_computation | async-start | bytes 8388608 | tf_op jit(solution)/shard_map/all_to_all | solution.py:84
where the time goes:
time: 376 us; the launch traced here: 374 us
  waiting for transfers between devices  90.8 us (24%)
  local copies, waits for them, and re-layouts  84.3 us (22%)
  matrix products  72.5 us (19%)
  blocking collectives  70.9 us (19%)
  other arithmetic  43.9 us (12%)
  starting transfers between devices  11.2 us (3%)
    all_to_all x1, waiting for transfers between devices, body(): lax.all_to_all(outgoing, 'ctx', split_axis=0, concat_axis=0, tiled=True)  90.8 us
    all_to_all x1, blocking collectives, body(): lax.all_to_all(attended, 'kvh', split_axis=0, concat_axis=1, tiled=True)  55.5 us
    dot_general x4, matrix products, block_attention(): jnp.einsum('gxqk,kgd->qgxd', weights, value_selection, preferred_element_...  38.9 us
    reduce_sum x4, other arithmetic, block_attention(): totals = jnp.sum(exponents, axis=-1, keepdims=True)  36.3 us
    dot_general x4, matrix products, block_attention(): jnp.einsum('qgxd,kgd->gxqk', query_heads, key_selection, preferred_elemen...  33.2 us
    dynamic_slice x12, local copies, waits for them, and re-layouts, body(): lax.map(attend_pair, (queries.reshape(blocks, BLOCK_TOKENS, -1), chosen))  23.2 us
    all_gather x1, blocking collectives, body(): pick_table = lax.all_gather(block_picks, 'ctx', axis=0, tiled=True)  15.4 us
    reshape x4, local copies, waits for them, and re-layouts, block_attention(): stacked = kv_block.reshape(pick_count * block_len, 2, kv_heads, HEAD_SIZE)  12.9 us
  transfers between devices with their start and end apart: 1, of which 1 were waited for; matrix products, arithmetic and copies ran while one was open for 0% of the time, Pallas kernels for 0%

commit v1 on v0

v1 whole, which is shorter than its diff:
```python
import functools
import math

import jax
import jax.numpy as jnp
from jax import lax
from jax.experimental import pallas as pl
from jax.experimental.pallas import tpu as pltpu
from jax.sharding import PartitionSpec as P

HEAD_SIZE = 128
BLOCK_TOKENS = 128
MESH = pl.DeviceIdType.MESH


def attend_kernel(n, parts, groups, blocks, picked, width, *refs):
    (req_ref, picks_ref, q_hbm, k_ref, v_ref, out_ref), rest = refs[:6], refs[6:]
    stages, rest = rest[:groups], rest[groups:]
    recvs, rest = rest[:groups], rest[groups:]
    (
        asked,
        asked_smem,
        q_ref,
        o_ref,
        k_sel,
        v_sel,
        ask_send,
        ask_recv,
        kv_send,
        kv_recv,
        out_send,
        out_recv,
        local_sem,
    ) = rest
    me = lax.axis_index("ctx")
    part = lax.axis_index("kvh")
    part_rows = out_ref.shape[0]
    chunk = min(BLOCK_TOKENS, part_rows)
    part_chunks = part_rows // chunk
    block_chunks = BLOCK_TOKENS // chunk
    cols = groups * width

    q_copy = pltpu.make_async_copy(q_hbm, q_ref, local_sem.at[0])
    q_copy.start()

    barrier = pltpu.get_barrier_semaphore()

    def greet_ctx(d, _):
        peer = lax.rem(me + d, n)
        pl.semaphore_signal(barrier, inc=1, device_id=(peer, part), device_id_type=MESH)
        return 0

    def greet_kvh(d, _):
        peer = lax.rem(part + d, parts)
        pl.semaphore_signal(barrier, inc=1, device_id=(me, peer), device_id_type=MESH)
        return 0

    lax.fori_loop(1, n, greet_ctx, 0)
    lax.fori_loop(1, parts, greet_kvh, 0)
    pl.semaphore_wait(barrier, n - 1 + parts - 1)

    def ask_copy(d):
        peer = lax.rem(me + d, n)
        return pltpu.make_async_remote_copy(
            src_ref=req_ref.at[peer],
            dst_ref=asked.at[n - 1 - d],
            send_sem=ask_send.at[d - 1],
            recv_sem=ask_recv.at[n - 1 - d],
            device_id=(peer, part),
            device_id_type=MESH,
        )

    def kv_copy(g, d):
        peer = lax.rem(me + d, n)
        return pltpu.make_async_remote_copy(
            src_ref=stages[g].at[d - 1],
            dst_ref=recvs[g].at[n - 1 - d],
            send_sem=kv_send.at[g, d - 1],
            recv_sem=kv_recv.at[g, n - 1 - d],
            device_id=(peer, part),
            device_id_type=MESH,
        )

    def over_peers(action):
        def one(d, _):
            action(d)
            return 0

        lax.fori_loop(1, n, one, 0)

    over_peers(lambda d: ask_copy(d).start())
    v_sel[:, HEAD_SIZE:] = jnp.ones((picked * BLOCK_TOKENS, HEAD_SIZE), jnp.bfloat16)
    over_peers(lambda d: ask_copy(d).wait_recv())
    to_smem = pltpu.make_async_copy(asked, asked_smem, local_sem.at[1])
    to_smem.start()
    to_smem.wait()

    def send_group(g):
        lanes = slice(g * HEAD_SIZE, (g + 1) * HEAD_SIZE)

        def one(d):
            wanted = asked_smem[d - 1, 0, 0]
            stages[g][d - 1, :BLOCK_TOKENS, :] = k_ref[wanted, :, lanes]
            stages[g][d - 1, BLOCK_TOKENS:, :] = v_ref[wanted, :, lanes]
            kv_copy(g, d).start()

        over_peers(one)

    for g in range(min(2, groups)):
        send_group(g)
    q_copy.wait()

    scale = math.log2(math.e) / math.sqrt(HEAD_SIZE)
    first_block = lax.rem(part + 1, parts) * part_rows // BLOCK_TOKENS

    def out_remote(g, index):
        target = index // part_chunks
        row = pl.multiple_of(lax.rem(index, part_chunks) * chunk, chunk)
        col = pl.multiple_of(part * cols + g * width, HEAD_SIZE)
        src_row = pl.multiple_of(index * chunk, chunk)
        src_col = pl.multiple_of(g * width, HEAD_SIZE)
        src = o_ref.at[pl.ds(src_row, chunk), pl.ds(src_col, width)]
        dst = out_ref.at[pl.ds(row, chunk), pl.ds(col, width)]
        slot = part * part_chunks + lax.rem(index, part_chunks)
        remote = pltpu.make_async_remote_copy(
            src_ref=src,
            dst_ref=dst,
            send_sem=out_send.at[g, index],
            recv_sem=out_recv.at[g, slot],
            device_id=(me, target),
            device_id_type=MESH,
        )
        local = pltpu.make_async_copy(src, dst, out_send.at[g, index])
        return target, remote, local

    def step(t, _):
        g = t // blocks
        turn = lax.rem(t, blocks)
        b = lax.rem(first_block + turn, blocks)
        for gi in range(groups):

            @pl.when(jnp.logical_and(g == gi, turn == 0))
            def _():
                over_peers(lambda d: kv_copy(gi, d).wait_recv())
                if gi + 2 < groups:
                    send_group(gi + 2)

            @pl.when(g == gi)
            def _():
                lanes = slice(gi * HEAD_SIZE, (gi + 1) * HEAD_SIZE)
                k_sel[:BLOCK_TOKENS, :] = k_ref[b, :, lanes]
                v_sel[:BLOCK_TOKENS, :HEAD_SIZE] = v_ref[b, :, lanes]
                for j in range(1, picked):
                    owner = picks_ref[b, j] // blocks
                    slot = jnp.minimum(lax.rem(owner + (n - 1) - me, n), n - 2)
                    rows = slice(j * BLOCK_TOKENS, (j + 1) * BLOCK_TOKENS)
                    k_sel[rows, :] = recvs[gi][slot, :BLOCK_TOKENS, :]
                    v_sel[rows, :HEAD_SIZE] = recvs[gi][slot, BLOCK_TOKENS:, :]

        q_rows = pl.ds(pl.multiple_of(b * BLOCK_TOKENS, BLOCK_TOKENS), BLOCK_TOKENS)
        heads = width // HEAD_SIZE
        pair = 2 if heads % 2 == 0 else 1
        row_id = lax.broadcasted_iota(jnp.int32, (pair * BLOCK_TOKENS, BLOCK_TOKENS), 0)
        key_id = lax.broadcasted_iota(jnp.int32, (pair * BLOCK_TOKENS, BLOCK_TOKENS), 1)
        causal = key_id <= lax.rem(row_id, BLOCK_TOKENS)
        for h in range(0, heads, pair):
            lanes = [
                pl.ds(pl.multiple_of(g * width + (h + u) * HEAD_SIZE, HEAD_SIZE), HEAD_SIZE)
                for u in range(pair)
            ]
            q = jnp.concatenate([q_ref[q_rows, lane] for lane in lanes], axis=0)
            scores = lax.dot_general(
                q, k_sel[...], (((1,), (1,)), ((), ())), preferred_element_type=jnp.float32
            )
            own = jnp.where(causal, scores[:, :BLOCK_TOKENS], -jnp.inf)
            scores = jnp.concatenate([own, scores[:, BLOCK_TOKENS:]], axis=1)
            top = jnp.max(scores, axis=1, keepdims=True)
            weights = jnp.exp2((scores - top) * scale).astype(jnp.bfloat16)
            both = jnp.dot(weights, v_sel[...], preferred_element_type=jnp.float32)
            result = (both[:, :HEAD_SIZE] / both[:, HEAD_SIZE:]).astype(jnp.bfloat16)
            for u in range(pair):
                o_ref[q_rows, lanes[u]] = result[u * BLOCK_TOKENS : (u + 1) * BLOCK_TOKENS]
        for c in range(block_chunks):
            target, remote, local = out_remote(g, b * block_chunks + c)

            @pl.when(target != part)
            def _():
                remote.start()

            @pl.when(target == part)
            def _():
                local.start()

        return 0

    lax.fori_loop(0, groups * blocks, step, 0)

    def finish(t, _):
        g = t // (parts * part_chunks)
        index = lax.rem(t, parts * part_chunks)
        target, remote, local = out_remote(g, index)

        @pl.when(target != part)
        def _():
            remote.wait_send()
            row = pl.multiple_of(lax.rem(index, part_chunks) * chunk, chunk)
            col = pl.multiple_of(target * cols + g * width, HEAD_SIZE)
            landed = out_ref.at[pl.ds(row, chunk), pl.ds(col, width)]
            pltpu.make_async_remote_copy(
                src_ref=landed,
                dst_ref=landed,
                send_sem=out_send.at[g, index],
                recv_sem=out_recv.at[g, index],
                device_id=(me, target),
                device_id_type=MESH,
            ).wait_recv()

        @pl.when(target == part)
        def _():
            local.wait()

        return 0

    over_peers(lambda d: ask_copy(d).wait_send())
    for g in range(groups):
        over_peers(lambda d: kv_copy(g, d).wait_send())
    lax.fori_loop(0, groups * parts * part_chunks, finish, 0)


def body(queries, key_vector_rows, value_vector_rows, block_picks):
    n = lax.axis_size("ctx")
    parts = lax.axis_size("kvh")
    tokens, cols = queries.shape
    blocks = tokens // BLOCK_TOKENS
    picked = block_picks.shape[1]
    groups = key_vector_rows.shape[1] // HEAD_SIZE
    width = cols // groups
    keys = key_vector_rows.reshape(blocks, BLOCK_TOKENS, groups * HEAD_SIZE)
    values = value_vector_rows.reshape(blocks, BLOCK_TOKENS, groups * HEAD_SIZE)
    remote = block_picks[:, 1:].reshape(-1)
    owned = (remote // blocks)[None, :] == jnp.arange(n, dtype=jnp.int32)[:, None]
    wanted = jnp.max(jnp.where(owned, (remote % blocks)[None, :], 0), axis=1)
    wanted = jnp.broadcast_to(wanted[:, None, None], (n, 1, 128))

    vmem = pl.BlockSpec(memory_space=pltpu.VMEM)
    anywhere = pl.BlockSpec(memory_space=pl.ANY)
    part_rows = tokens // parts
    chunks = tokens // min(BLOCK_TOKENS, part_rows)
    slots = pltpu.VMEM((n - 1, 2 * BLOCK_TOKENS, HEAD_SIZE), jnp.bfloat16)
    return pl.pallas_call(
        functools.partial(attend_kernel, n, parts, groups, blocks, picked, width),
        out_shape=jax.ShapeDtypeStruct((part_rows, parts * cols), jnp.bfloat16),
        in_specs=[vmem, pl.BlockSpec(memory_space=pltpu.SMEM), anywhere, vmem, vmem],
        out_specs=anywhere,
        scratch_shapes=[slots] * (2 * groups)
        + [
            pltpu.VMEM((n - 1, 1, 128), jnp.int32),
            pltpu.SMEM((n - 1, 1, 128), jnp.int32),
            pltpu.VMEM((tokens, cols), jnp.bfloat16),
            pltpu.VMEM((tokens, cols), jnp.bfloat16),
            pltpu.VMEM((picked * BLOCK_TOKENS, HEAD_SIZE), jnp.bfloat16),
            pltpu.VMEM((picked * BLOCK_TOKENS, 2 * HEAD_SIZE), jnp.bfloat16),
            pltpu.SemaphoreType.DMA((n - 1,)),
            pltpu.SemaphoreType.DMA((n - 1,)),
            pltpu.SemaphoreType.DMA((groups, n - 1)),
            pltpu.SemaphoreType.DMA((groups, n - 1)),
            pltpu.SemaphoreType.DMA((groups, chunks)),
            pltpu.SemaphoreType.DMA((groups, chunks)),
            pltpu.SemaphoreType.DMA((2,)),
        ],
        compiler_params=pltpu.CompilerParams(
            collective_id=0, has_side_effects=True, vmem_limit_bytes=48 * 2**20
        ),
        cost_estimate=pl.CostEstimate(
            flops=4 * tokens * cols * picked * BLOCK_TOKENS,
            bytes_accessed=4 * tokens * cols,
            transcendentals=tokens * (cols // HEAD_SIZE) * picked * BLOCK_TOKENS,
        ),
    )(wanted, block_picks, queries, keys, values)


def solution(mesh):
    return jax.shard_map(
        body,
        mesh=mesh,
        in_specs=(P("ctx", "kvh"), P("ctx", "kvh"), P("ctx", "kvh"), P("ctx", None)),
        out_specs=P(("ctx", "kvh"), None),
        check_vma=False,
    )
```

time: 376 us -> 124 us (0.33)
  the two profiles are of different devices: /device:TPU:10 before, /device:TPU:11 now
where the time goes in v1:
time: 124 us; the launch traced here: 123 us
  Pallas kernels  118 us (95%)
  local copies, waits for them, and re-layouts  5.7 us (5%)
    pallas_call x1, Pallas kernels, body(): pl.pallas_call(functools.partial(attend_kernel, n, parts, groups, blocks,...  118 us
    unnamed x7, local copies, waits for them, and re-layouts  4.79 us

profile of v1, /device:TPU:11, one launch (start us, length us, event | category | flops | bytes accessed | tf_op | source)
XLA Modules:
  0.0 123.4 jit_solution(14563374759174482531)
XLA Ops:
  0.0 0.8 slice.3
  0.8 0.1 reshape.61
  0.9 0.1 select_reduce_fusion
  1.0 0.1 broadcast_in_dim.23.refs_0_
  1.0 0.0 copy-start
  1.1 0.7 copy-done
  1.7 0.0 copy-start.1
  1.7 1.0 copy-done.1
  2.8 0.0 copy-start.2
  2.8 1.0 copy-done.2
  3.8 117.6 %shard_map.46 = bf16[256,8192]{1,0:T(8,128)(2,1)S(1)} custom-call(s32[16,1,128]{2,1,0:T(1,128)S(1)} %broadcast_in_dim.23.refs_0_, s32[4,8]{1,0:T(4,128)S(1)} %copy-done, bf16[512,4096]{1,0:T(8,128)(2,1)} %refs_2_.1, bf16[4,128,512]{2,1,0:T(8,128)(2,1)S(1)} %bitcast.2, bf16[4,128,512]{2,1,0:T(8,128)(2,1)S(1)} %bitcast.3), custom_call_target="tpu_custom_call" | custom-call | flops 8589934592 | bytes 8388608 | tf_op jit(solution)/shard_map/pallas_call | solution.py:250
  121.4 2.0 %copy.6 = bf16[256,8192]{1,0:T(8,128)(2,1)} copy(bf16[256,8192]{1,0:T(8,128)(2,1)S(1)} %shard_map.46) | data formatting | bytes 8388608
  (1 shorter events, 0.0 us)
Async XLA Ops:
  1.0 0.7 copy-start
  1.7 1.0 copy-start.1
  2.8 1.0 copy-start.2

commit v2 on v1

--- a/solution.py
+++ b/solution.py
@@ -13,10 +13,13 @@
 MESH = pl.DeviceIdType.MESH
 
 
-def attend_kernel(n, parts, groups, blocks, picked, width, *refs):
+def attend_kernel(n, line, parts, groups, blocks, picked, width, *refs):
     (req_ref, picks_ref, q_hbm, k_ref, v_ref, out_ref), rest = refs[:6], refs[6:]
+    owns, rest = rest[:groups], rest[groups:]
+    from_left, rest = rest[: groups * (line - 1)], rest[groups * (line - 1) :]
+    from_right, rest = rest[: groups * (line - 1)], rest[groups * (line - 1) :]
     stages, rest = rest[:groups], rest[groups:]
-    recvs, rest = rest[:groups], rest[groups:]
+    chosen, rest = rest[:groups], rest[groups:]
     (
         asked,
         asked_smem,
@@ -26,14 +29,20 @@
         v_sel,
         ask_send,
         ask_recv,
-        kv_send,
-        kv_recv,
+        right_send,
+        left_recv,
+        left_send,
+        right_recv,
+        plane_send,
+        plane_recv,
         out_send,
         out_recv,
         local_sem,
     ) = rest
     me = lax.axis_index("ctx")
     part = lax.axis_index("kvh")
+    plane = n // line
+    place, seat = me // plane, lax.rem(me, plane)
     part_rows = out_ref.shape[0]
     chunk = min(BLOCK_TOKENS, part_rows)
     part_chunks = part_rows // chunk
@@ -57,57 +66,141 @@
 
     lax.fori_loop(1, n, greet_ctx, 0)
     lax.fori_loop(1, parts, greet_kvh, 0)
+
+    def pack(g):
+        lanes = slice(g * HEAD_SIZE, (g + 1) * HEAD_SIZE)
+        for i in range(blocks):
+            owns[g][i, :BLOCK_TOKENS, :] = k_ref[i, :, lanes]
+            owns[g][i, BLOCK_TOKENS:, :] = v_ref[i, :, lanes]
+
+    for g in range(groups):
+        pack(g)
+    asked[plane - 1] = req_ref[...]
+    v_sel[:, HEAD_SIZE:] = jnp.ones((picked * BLOCK_TOKENS, HEAD_SIZE), jnp.bfloat16)
     pl.semaphore_wait(barrier, n - 1 + parts - 1)
-
-    def ask_copy(d):
-        peer = lax.rem(me + d, n)
-        return pltpu.make_async_remote_copy(
-            src_ref=req_ref.at[peer],
-            dst_ref=asked.at[n - 1 - d],
-            send_sem=ask_send.at[d - 1],
-            recv_sem=ask_recv.at[n - 1 - d],
-            device_id=(peer, part),
-            device_id_type=MESH,
-        )
-
-    def kv_copy(g, d):
-        peer = lax.rem(me + d, n)
-        return pltpu.make_async_remote_copy(
-            src_ref=stages[g].at[d - 1],
-            dst_ref=recvs[g].at[n - 1 - d],
-            send_sem=kv_send.at[g, d - 1],
-            recv_sem=kv_recv.at[g, n - 1 - d],
-            device_id=(peer, part),
-            device_id_type=MESH,
-        )
 
     def over_peers(action):
         def one(d, _):
             action(d)
             return 0
 
-        lax.fori_loop(1, n, one, 0)
+        lax.fori_loop(1, plane, one, 0)
+
+    def plane_peer(d):
+        return (place * plane + lax.rem(seat + d, plane), part)
+
+    def ask_copy(d):
+        return pltpu.make_async_remote_copy(
+            src_ref=req_ref,
+            dst_ref=asked.at[plane - 1 - d],
+            send_sem=ask_send.at[d - 1],
+            recv_sem=ask_recv.at[plane - 1 - d],
+            device_id=plane_peer(d),
+            device_id_type=MESH,
+        )
+
+    def right_copy(g, k):
+        return pltpu.make_async_remote_copy(
+            src_ref=owns[g] if k == 0 else from_left[g * (line - 1) + k - 1],
+            dst_ref=from_left[g * (line - 1) + k],
+            send_sem=right_send.at[g, k],
+            recv_sem=left_recv.at[g, k],
+            device_id=(me + plane, part),
+            device_id_type=MESH,
+        )
+
+    def left_copy(g, k):
+        return pltpu.make_async_remote_copy(
+            src_ref=owns[g] if k == 0 else from_right[g * (line - 1) + k - 1],
+            dst_ref=from_right[g * (line - 1) + k],
+            send_sem=left_send.at[g, k],
+            recv_sem=right_recv.at[g, k],
+            device_id=(me - plane, part),
+            device_id_type=MESH,
+        )
+
+    def plane_copy(g, d, source):
+        return pltpu.make_async_remote_copy(
+            src_ref=stages[g].at[d - 1, source],
+            dst_ref=chosen[g].at[plane - 1 - d, source],
+            send_sem=plane_send.at[g, d - 1, source],
+            recv_sem=plane_recv.at[g, plane - 1 - d, source],
+            device_id=plane_peer(d),
+            device_id_type=MESH,
+        )
+
+    def share(g, shard, source):
+        owner = source * plane + seat
+
+        def one(d):
+            wanted = asked_smem[d - 1, 0, owner]
+            stages[g][d - 1, source] = shard[wanted]
+            plane_copy(g, d, source).start()
+
+        over_peers(one)
+        chosen[g][plane - 1, source] = shard[asked_smem[plane - 1, 0, owner]]
+
+    def begin(g):
+        @pl.when(place < line - 1)
+        def _():
+            right_copy(g, 0).start()
+
+        @pl.when(place > 0)
+        def _():
+            left_copy(g, 0).start()
+
+    def hop(g, k):
+        last = line - 1
+
+        @pl.when(place >= k)
+        def _():
+            right_copy(g, k - 1).wait_recv()
+            if k < last:
+
+                @pl.when(place < last)
+                def _():
+                    right_copy(g, k).start()
+
+        @pl.when(place + k <= last)
+        def _():
+            left_copy(g, k - 1).wait_recv()
+            if k < last:
+
+                @pl.when(place > 0)
+                def _():
+                    left_copy(g, k).start()
+
+        if k == 1 and g + 1 < groups:
+            begin(g + 1)
+            share(g + 1, owns[g + 1], place)
+
+        @pl.when(place >= k)
+        def _():
+            share(g, from_left[g * (line - 1) + k - 1], place - k)
+
+        @pl.when(place + k <= last)
+        def _():
+            share(g, from_right[g * (line - 1) + k - 1], place + k)
+
+    def wait_chosen(g):
+        def one(d):
+            def source(i, _):
+                plane_copy(g, d, i).wait_recv()
+                return 0
+
+            lax.fori_loop(0, line, source, 0)
+
+        over_peers(one)
 
     over_peers(lambda d: ask_copy(d).start())
-    v_sel[:, HEAD_SIZE:] = jnp.ones((picked * BLOCK_TOKENS, HEAD_SIZE), jnp.bfloat16)
+    begin(0)
     over_peers(lambda d: ask_copy(d).wait_recv())
     to_smem = pltpu.make_async_copy(asked, asked_smem, local_sem.at[1])
     to_smem.start()
     to_smem.wait()
-
-    def send_group(g):
-        lanes = slice(g * HEAD_SIZE, (g + 1) * HEAD_SIZE)
-
-        def one(d):
-            wanted = asked_smem[d - 1, 0, 0]
-            stages[g][d - 1, :BLOCK_TOKENS, :] = k_ref[wanted, :, lanes]
-            stages[g][d - 1, BLOCK_TOKENS:, :] = v_ref[wanted, :, lanes]
-            kv_copy(g, d).start()
-
-        over_peers(one)
-
-    for g in range(min(2, groups)):
-        send_group(g)
+    share(0, owns[0], place)
+    for k in range(1, line):
+        hop(0, k)
     q_copy.wait()
 
     scale = math.log2(math.e) / math.sqrt(HEAD_SIZE)
@@ -133,17 +226,25 @@
         local = pltpu.make_async_copy(src, dst, out_send.at[g, index])
         return target, remote, local
 
+    hop_turn = {k: (k - 1) * blocks // (line - 1) + (1 if k > 1 else 0) for k in range(1, line)}
+    hop_turn = {k: min(turn, blocks - 1) for k, turn in hop_turn.items()}
+
     def step(t, _):
         g = t // blocks
         turn = lax.rem(t, blocks)
         b = lax.rem(first_block + turn, blocks)
         for gi in range(groups):
-
-            @pl.when(jnp.logical_and(g == gi, turn == 0))
-            def _():
-                over_peers(lambda d: kv_copy(gi, d).wait_recv())
-                if gi + 2 < groups:
-                    send_group(gi + 2)
+            for ti in range(blocks):
+                hops = [k for k in range(1, line) if hop_turn[k] == ti and gi + 1 < groups]
+                if not hops and ti > 0:
+                    continue
+
+                @pl.when(jnp.logical_and(g == gi, turn == ti))
+                def _():
+                    for k in hops:
+                        hop(gi + 1, k)
+                    if ti == 0:
+                        wait_chosen(gi)
 
             @pl.when(g == gi)
             def _():
@@ -152,10 +253,10 @@
                 v_sel[:BLOCK_TOKENS, :HEAD_SIZE] = v_ref[b, :, lanes]
                 for j in range(1, picked):
                     owner = picks_ref[b, j] // blocks
-                    slot = jnp.minimum(lax.rem(owner + (n - 1) - me, n), n - 2)
+                    slot = lax.rem(lax.rem(owner, plane) + (plane - 1) - seat + plane, plane)
                     rows = slice(j * BLOCK_TOKENS, (j + 1) * BLOCK_TOKENS)
-                    k_sel[rows, :] = recvs[gi][slot, :BLOCK_TOKENS, :]
-                    v_sel[rows, :HEAD_SIZE] = recvs[gi][slot, BLOCK_TOKENS:, :]
+                    k_sel[rows, :] = chosen[gi][slot, owner // plane, :BLOCK_TOKENS, :]
+                    v_sel[rows, :HEAD_SIZE] = chosen[gi][slot, owner // plane, BLOCK_TOKENS:, :]
 
         q_rows = pl.ds(pl.multiple_of(b * BLOCK_TOKENS, BLOCK_TOKENS), BLOCK_TOKENS)
         heads = width // HEAD_SIZE
@@ -221,13 +322,32 @@
 
         return 0
 
+    def plane_done(d):
+        for g in range(groups):
+
+            def source(i, _):
+                plane_copy(g, d, i).wait_send()
+                return 0
+
+            lax.fori_loop(0, line, source, 0)
+
     over_peers(lambda d: ask_copy(d).wait_send())
+    over_peers(plane_done)
     for g in range(groups):
-        over_peers(lambda d: kv_copy(g, d).wait_send())
+        for k in range(line - 1):
+
+            @pl.when(jnp.logical_and(place < line - 1, place >= k))
+            def _():
+                right_copy(g, k).wait_send()
+
+            @pl.when(jnp.logical_and(place > 0, place + k <= line - 1))
+            def _():
+                left_copy(g, k).wait_send()
+
     lax.fori_loop(0, groups * parts * part_chunks, finish, 0)
 
 
-def body(queries, key_vector_rows, value_vector_rows, block_picks):
+def body(line, queries, key_vector_rows, value_vector_rows, block_picks):
     n = lax.axis_size("ctx")
     parts = lax.axis_size("kvh")
     tokens, cols = queries.shape
@@ -240,30 +360,40 @@
     remote = block_picks[:, 1:].reshape(-1)
     owned = (remote // blocks)[None, :] == jnp.arange(n, dtype=jnp.int32)[:, None]
     wanted = jnp.max(jnp.where(owned, (remote % blocks)[None, :], 0), axis=1)
-    wanted = jnp.broadcast_to(wanted[:, None, None], (n, 1, 128))
+    lanes = -(-n // 128) * 128
+    wanted = jnp.pad(wanted, (0, lanes - n)).reshape(1, lanes)
 
     vmem = pl.BlockSpec(memory_space=pltpu.VMEM)
     anywhere = pl.BlockSpec(memory_space=pl.ANY)
     part_rows = tokens // parts
     chunks = tokens // min(BLOCK_TOKENS, part_rows)
-    slots = pltpu.VMEM((n - 1, 2 * BLOCK_TOKENS, HEAD_SIZE), jnp.bfloat16)
+    plane = n // line
+    shard = pltpu.VMEM((blocks, 2 * BLOCK_TOKENS, HEAD_SIZE), jnp.bfloat16)
+    stage = pltpu.VMEM((plane - 1, line, 2 * BLOCK_TOKENS, HEAD_SIZE), jnp.bfloat16)
+    slots = pltpu.VMEM((plane, line, 2 * BLOCK_TOKENS, HEAD_SIZE), jnp.bfloat16)
     return pl.pallas_call(
-        functools.partial(attend_kernel, n, parts, groups, blocks, picked, width),
+        functools.partial(attend_kernel, n, line, parts, groups, blocks, picked, width),
         out_shape=jax.ShapeDtypeStruct((part_rows, parts * cols), jnp.bfloat16),
         in_specs=[vmem, pl.BlockSpec(memory_space=pltpu.SMEM), anywhere, vmem, vmem],
         out_specs=anywhere,
-        scratch_shapes=[slots] * (2 * groups)
+        scratch_shapes=[shard] * (groups * (2 * line - 1))
+        + [stage] * groups
+        + [slots] * groups
         + [
-            pltpu.VMEM((n - 1, 1, 128), jnp.int32),
-            pltpu.SMEM((n - 1, 1, 128), jnp.int32),
+            pltpu.VMEM((plane, 1, lanes), jnp.int32),
+            pltpu.SMEM((plane, 1, lanes), jnp.int32),
             pltpu.VMEM((tokens, cols), jnp.bfloat16),
             pltpu.VMEM((tokens, cols), jnp.bfloat16),
             pltpu.VMEM((picked * BLOCK_TOKENS, HEAD_SIZE), jnp.bfloat16),
             pltpu.VMEM((picked * BLOCK_TOKENS, 2 * HEAD_SIZE), jnp.bfloat16),
-            pltpu.SemaphoreType.DMA((n - 1,)),
-            pltpu.SemaphoreType.DMA((n - 1,)),
-            pltpu.SemaphoreType.DMA((groups, n - 1)),
-            pltpu.SemaphoreType.DMA((groups, n - 1)),
+            pltpu.SemaphoreType.DMA((plane - 1,)),
+            pltpu.SemaphoreType.DMA((plane - 1,)),
+            pltpu.SemaphoreType.DMA((groups, line)),
+            pltpu.SemaphoreType.DMA((groups, line)),
+            pltpu.SemaphoreType.DMA((groups, line)),
+            pltpu.SemaphoreType.DMA((groups, line)),
+            pltpu.SemaphoreType.DMA((groups, plane - 1, line)),
+            pltpu.SemaphoreType.DMA((groups, plane - 1, line)),
             pltpu.SemaphoreType.DMA((groups, chunks)),
             pltpu.SemaphoreType.DMA((groups, chunks)),
             pltpu.SemaphoreType.DMA((2,)),
@@ -279,9 +409,23 @@
     )(wanted, block_picks, queries, keys, values)
 
 
+def line_length(mesh):
+    n = mesh.shape["ctx"]
+    column = mesh.devices.reshape(n, -1)[:, 0]
+    places = [getattr(device, "coords", None) for device in column]
+    if places[0] is not None:
+        firsts = [
+            next((i for i in range(n) if places[i][axis] != places[0][axis]), 0)
+            for axis in range(len(places[0]))
+        ]
+        if 1 < max(firsts) < n and n % max(firsts) == 0:
+            return n // max(firsts)
+    return next(a for a in range(math.isqrt(n), 0, -1) if n % a == 0)
+
+
 def solution(mesh):
     return jax.shard_map(
-        body,
+        functools.partial(body, line_length(mesh)),
         mesh=mesh,
         in_specs=(P("ctx", "kvh"), P("ctx", "kvh"), P("ctx", "kvh"), P("ctx", None)),
         out_specs=P(("ctx", "kvh"), None),

time: 124 us -> 106 us (0.85)
  the two profiles are of different devices: /device:TPU:11 before, /device:TPU:0 now
where the time goes in v2:
time: 106 us; the launch traced here: 105 us
  Pallas kernels  99.6 us (94%)
  local copies, waits for them, and re-layouts  5.62 us (5%)
    pallas_call x1, Pallas kernels, body(): pl.pallas_call(functools.partial(attend_kernel, n, line, parts, groups, b...  99.6 us
    unnamed x7, local copies, waits for them, and re-layouts  4.77 us

profile of v2, /device:TPU:0, one launch (start us, length us, event | category | flops | bytes accessed | tf_op | source)
XLA Modules:
  0.0 105.4 jit_solution(11726799819075862436)
XLA Ops:
  0.0 0.8 slice.3
  0.8 0.1 reshape.61
  0.9 0.1 select_reduce_fusion
  1.0 0.0 copy-start
  1.0 0.7 copy-done
  1.7 0.0 copy-start.1
  1.7 1.0 copy-done.1
  2.7 0.0 copy-start.2
  2.7 1.0 copy-done.2
  3.8 99.6 %shard_map.46 = bf16[256,8192]{1,0:T(8,128)(2,1)S(1)} custom-call(s32[1,128]{1,0:T(1,128)S(1)} %pad_bitcast_fusion.refs_0_, s32[4,8]{1,0:T(4,128)S(1)} %copy-done, bf16[512,4096]{1,0:T(8,128)(2,1)} %refs_2_.1, bf16[4,128,512]{2,1,0:T(8,128)(2,1)S(1)} %bitcast.4, bf16[4,128,512]{2,1,0:T(8,128)(2,1)S(1)} %bitcast.5), custom_call_target="tpu_custom_call" | custom-call | flops 8589934592 | bytes 8388608 | tf_op jit(solution)/shard_map/pallas_call | solution.py:374
  103.3 2.0 %copy.6 = bf16[256,8192]{1,0:T(8,128)(2,1)} copy(bf16[256,8192]{1,0:T(8,128)(2,1)S(1)} %shard_map.46) | data formatting | bytes 8388608
  (2 shorter events, 0.0 us)
Async XLA Ops:
  1.0 0.7 copy-start
  1.7 1.0 copy-start.1
  2.7 1.0 copy-start.2

commit v3 on v2

--- a/solution.py
+++ b/solution.py
@@ -14,7 +14,7 @@
 
 
 def attend_kernel(n, line, parts, groups, blocks, picked, width, *refs):
-    (req_ref, picks_ref, q_hbm, k_ref, v_ref, out_ref), rest = refs[:6], refs[6:]
+    (req_ref, picks_ref, q_hbm, k_hbm, v_hbm, out_ref), rest = refs[:6], refs[6:]
     owns, rest = rest[:groups], rest[groups:]
     from_left, rest = rest[: groups * (line - 1)], rest[groups * (line - 1) :]
     from_right, rest = rest[: groups * (line - 1)], rest[groups * (line - 1) :]
@@ -24,6 +24,8 @@
         asked,
         asked_smem,
         q_ref,
+        k_ref,
+        v_ref,
         o_ref,
         k_sel,
         v_sel,
@@ -49,7 +51,11 @@
     block_chunks = BLOCK_TOKENS // chunk
     cols = groups * width
 
+    k_copy = pltpu.make_async_copy(k_hbm, k_ref, local_sem.at[2])
+    v_copy = pltpu.make_async_copy(v_hbm, v_ref, local_sem.at[3])
     q_copy = pltpu.make_async_copy(q_hbm, q_ref, local_sem.at[0])
+    k_copy.start()
+    v_copy.start()
     q_copy.start()
 
     barrier = pltpu.get_barrier_semaphore()
@@ -73,10 +79,12 @@
             owns[g][i, :BLOCK_TOKENS, :] = k_ref[i, :, lanes]
             owns[g][i, BLOCK_TOKENS:, :] = v_ref[i, :, lanes]
 
+    asked[plane - 1] = req_ref[...]
+    v_sel[:, HEAD_SIZE:] = jnp.ones((picked * BLOCK_TOKENS, HEAD_SIZE), jnp.bfloat16)
+    k_copy.wait()
+    v_copy.wait()
     for g in range(groups):
         pack(g)
-    asked[plane - 1] = req_ref[...]
-    v_sel[:, HEAD_SIZE:] = jnp.ones((picked * BLOCK_TOKENS, HEAD_SIZE), jnp.bfloat16)
     pl.semaphore_wait(barrier, n - 1 + parts - 1)
 
     def over_peers(action):
@@ -264,23 +272,46 @@
         row_id = lax.broadcasted_iota(jnp.int32, (pair * BLOCK_TOKENS, BLOCK_TOKENS), 0)
         key_id = lax.broadcasted_iota(jnp.int32, (pair * BLOCK_TOKENS, BLOCK_TOKENS), 1)
         causal = key_id <= lax.rem(row_id, BLOCK_TOKENS)
+        span = picked * BLOCK_TOKENS
+        tile = 2 * BLOCK_TOKENS if span % (2 * BLOCK_TOKENS) == 0 else BLOCK_TOKENS
+
+        def lanes_of(h):
+            start = pl.multiple_of(g * width + h * HEAD_SIZE, HEAD_SIZE)
+            return pl.ds(start, HEAD_SIZE)
+
+        def load_queries(h):
+            return jnp.concatenate([q_ref[q_rows, lanes_of(h + u)] for u in range(pair)], axis=0)
+
+        def score_tile(q, start):
+            keys = k_sel[start : start + tile, :]
+            scores = lax.dot_general(
+                q, keys, (((1,), (1,)), ((), ())), preferred_element_type=jnp.float32
+            )
+            if start == 0:
+                own = jnp.where(causal, scores[:, :BLOCK_TOKENS], -jnp.inf)
+                scores = jnp.concatenate([own, scores[:, BLOCK_TOKENS:]], axis=1)
+            return scores
+
+        starts = range(0, span, tile)
+        q = load_queries(0)
+        tiles = [score_tile(q, start) for start in starts]
         for h in range(0, heads, pair):
-            lanes = [
-                pl.ds(pl.multiple_of(g * width + (h + u) * HEAD_SIZE, HEAD_SIZE), HEAD_SIZE)
-                for u in range(pair)
-            ]
-            q = jnp.concatenate([q_ref[q_rows, lane] for lane in lanes], axis=0)
-            scores = lax.dot_general(
-                q, k_sel[...], (((1,), (1,)), ((), ())), preferred_element_type=jnp.float32
-            )
-            own = jnp.where(causal, scores[:, :BLOCK_TOKENS], -jnp.inf)
-            scores = jnp.concatenate([own, scores[:, BLOCK_TOKENS:]], axis=1)
-            top = jnp.max(scores, axis=1, keepdims=True)
-            weights = jnp.exp2((scores - top) * scale).astype(jnp.bfloat16)
+            top = functools.reduce(jnp.maximum, tiles)
+            top = jnp.max(top, axis=1, keepdims=True)
+            more = h + pair < heads
+            if more:
+                q = load_queries(h + pair)
+            weights, following = [], []
+            for scores, start in zip(tiles, starts):
+                if more:
+                    following.append(score_tile(q, start))
+                weights.append(jnp.exp2((scores - top) * scale).astype(jnp.bfloat16))
+            weights = jnp.concatenate(weights, axis=1)
             both = jnp.dot(weights, v_sel[...], preferred_element_type=jnp.float32)
             result = (both[:, :HEAD_SIZE] / both[:, HEAD_SIZE:]).astype(jnp.bfloat16)
             for u in range(pair):
-                o_ref[q_rows, lanes[u]] = result[u * BLOCK_TOKENS : (u + 1) * BLOCK_TOKENS]
+                o_ref[q_rows, lanes_of(h + u)] = result[u * BLOCK_TOKENS : (u + 1) * BLOCK_TOKENS]
+            tiles = following
         for c in range(block_chunks):
             target, remote, local = out_remote(g, b * block_chunks + c)
 
@@ -374,7 +405,7 @@
     return pl.pallas_call(
         functools.partial(attend_kernel, n, line, parts, groups, blocks, picked, width),
         out_shape=jax.ShapeDtypeStruct((part_rows, parts * cols), jnp.bfloat16),
-        in_specs=[vmem, pl.BlockSpec(memory_space=pltpu.SMEM), anywhere, vmem, vmem],
+        in_specs=[vmem, pl.BlockSpec(memory_space=pltpu.SMEM), anywhere, anywhere, anywhere],
         out_specs=anywhere,
         scratch_shapes=[shard] * (groups * (2 * line - 1))
         + [stage] * groups
@@ -383,6 +414,8 @@
             pltpu.VMEM((plane, 1, lanes), jnp.int32),
             pltpu.SMEM((plane, 1, lanes), jnp.int32),
             pltpu.VMEM((tokens, cols), jnp.bfloat16),
+            pltpu.VMEM(keys.shape, jnp.bfloat16),
+            pltpu.VMEM(values.shape, jnp.bfloat16),
             pltpu.VMEM((tokens, cols), jnp.bfloat16),
             pltpu.VMEM((picked * BLOCK_TOKENS, HEAD_SIZE), jnp.bfloat16),
             pltpu.VMEM((picked * BLOCK_TOKENS, 2 * HEAD_SIZE), jnp.bfloat16),
@@ -396,7 +429,7 @@
             pltpu.SemaphoreType.DMA((groups, plane - 1, line)),
             pltpu.SemaphoreType.DMA((groups, chunks)),
             pltpu.SemaphoreType.DMA((groups, chunks)),
-            pltpu.SemaphoreType.DMA((2,)),
+            pltpu.SemaphoreType.DMA((4,)),
         ],
         compiler_params=pltpu.CompilerParams(
             collective_id=0, has_side_effects=True, vmem_limit_bytes=48 * 2**20

time: 106 us -> 105 us (level)
  no operation moved by 1% of the time
where the time goes in v3:
time: 105 us
  Pallas kernels  99.5 us (95%)
  local copies, waits for them, and re-layouts  5.62 us (5%)
    pallas_call x1, Pallas kernels, body(): pl.pallas_call(functools.partial(attend_kernel, n, line, parts, groups, b...  99.5 us
    unnamed x7, local copies, waits for them, and re-layouts  4.77 us

profile of v3, /device:TPU:0, one launch (start us, length us, event | category | flops | bytes accessed | tf_op | source)
XLA Modules:
  0.0 105.2 jit_solution(349542287620914652)
XLA Ops:
  0.0 0.8 slice.3
  0.8 0.1 reshape.61
  0.9 0.1 select_reduce_fusion
  1.0 0.0 copy-start
  1.0 0.7 copy-done
  1.7 0.0 copy-start.1
  1.7 1.0 copy-done.1
  2.7 0.0 copy-start.2
  2.7 1.0 copy-done.2
  3.8 99.5 %shard_map.46 = bf16[256,8192]{1,0:T(8,128)(2,1)S(1)} custom-call(s32[1,128]{1,0:T(1,128)S(1)} %pad_bitcast_fusion.refs_0_, s32[4,8]{1,0:T(4,128)S(1)} %copy-done, bf16[512,4096]{1,0:T(8,128)(2,1)} %refs_2_.1, bf16[4,128,512]{2,1,0:T(8,128)(2,1)S(1)} %bitcast.4, bf16[4,128,512]{2,1,0:T(8,128)(2,1)S(1)} %bitcast.5), custom_call_target="tpu_custom_call" | custom-call | flops 8589934592 | bytes 8388608 | tf_op jit(solution)/shard_map/pallas_call | solution.py:405
  103.2 2.0 %copy.6 = bf16[256,8192]{1,0:T(8,128)(2,1)} copy(bf16[256,8192]{1,0:T(8,128)(2,1)S(1)} %shard_map.46) | data formatting | bytes 8388608
  (2 shorter events, 0.0 us)
Async XLA Ops:
  1.0 0.7 copy-start
  1.7 1.0 copy-start.1
  2.7 1.0 copy-start.2

commit v4 on v3

--- a/solution.py
+++ b/solution.py
@@ -76,15 +76,15 @@
     def pack(g):
         lanes = slice(g * HEAD_SIZE, (g + 1) * HEAD_SIZE)
         for i in range(blocks):
-            owns[g][i, :BLOCK_TOKENS, :] = k_ref[i, :, lanes]
-            owns[g][i, BLOCK_TOKENS:, :] = v_ref[i, :, lanes]
+            keys = k_ref[i, :, lanes].astype(jnp.float32).T
+            owns[g][i, :HEAD_SIZE, :] = keys.astype(jnp.bfloat16)
+            owns[g][i, HEAD_SIZE:, :] = v_ref[i, :, lanes]
 
     asked[plane - 1] = req_ref[...]
     v_sel[:, HEAD_SIZE:] = jnp.ones((picked * BLOCK_TOKENS, HEAD_SIZE), jnp.bfloat16)
     k_copy.wait()
     v_copy.wait()
-    for g in range(groups):
-        pack(g)
+    pack(0)
     pl.semaphore_wait(barrier, n - 1 + parts - 1)
 
     def over_peers(action):
@@ -179,6 +179,7 @@
                     left_copy(g, k).start()
 
         if k == 1 and g + 1 < groups:
+            pack(g + 1)
             begin(g + 1)
             share(g + 1, owns[g + 1], place)
 
@@ -256,15 +257,14 @@
 
             @pl.when(g == gi)
             def _():
-                lanes = slice(gi * HEAD_SIZE, (gi + 1) * HEAD_SIZE)
-                k_sel[:BLOCK_TOKENS, :] = k_ref[b, :, lanes]
-                v_sel[:BLOCK_TOKENS, :HEAD_SIZE] = v_ref[b, :, lanes]
+                k_sel[:, :BLOCK_TOKENS] = owns[gi][b, :HEAD_SIZE, :]
+                v_sel[:BLOCK_TOKENS, :HEAD_SIZE] = owns[gi][b, HEAD_SIZE:, :]
                 for j in range(1, picked):
                     owner = picks_ref[b, j] // blocks
                     slot = lax.rem(lax.rem(owner, plane) + (plane - 1) - seat + plane, plane)
                     rows = slice(j * BLOCK_TOKENS, (j + 1) * BLOCK_TOKENS)
-                    k_sel[rows, :] = chosen[gi][slot, owner // plane, :BLOCK_TOKENS, :]
-                    v_sel[rows, :HEAD_SIZE] = chosen[gi][slot, owner // plane, BLOCK_TOKENS:, :]
+                    k_sel[:, rows] = chosen[gi][slot, owner // plane, :HEAD_SIZE, :]
+                    v_sel[rows, :HEAD_SIZE] = chosen[gi][slot, owner // plane, HEAD_SIZE:, :]
 
         q_rows = pl.ds(pl.multiple_of(b * BLOCK_TOKENS, BLOCK_TOKENS), BLOCK_TOKENS)
         heads = width // HEAD_SIZE
@@ -283,10 +283,8 @@
             return jnp.concatenate([q_ref[q_rows, lanes_of(h + u)] for u in range(pair)], axis=0)
 
         def score_tile(q, start):
-            keys = k_sel[start : start + tile, :]
-            scores = lax.dot_general(
-                q, keys, (((1,), (1,)), ((), ())), preferred_element_type=jnp.float32
-            )
+            keys = k_sel[:, start : start + tile]
+            scores = jnp.dot(q, keys, preferred_element_type=jnp.float32)
             if start == 0:
                 own = jnp.where(causal, scores[:, :BLOCK_TOKENS], -jnp.inf)
                 scores = jnp.concatenate([own, scores[:, BLOCK_TOKENS:]], axis=1)
@@ -388,9 +386,8 @@
     width = cols // groups
     keys = key_vector_rows.reshape(blocks, BLOCK_TOKENS, groups * HEAD_SIZE)
     values = value_vector_rows.reshape(blocks, BLOCK_TOKENS, groups * HEAD_SIZE)
-    remote = block_picks[:, 1:].reshape(-1)
-    owned = (remote // blocks)[None, :] == jnp.arange(n, dtype=jnp.int32)[:, None]
-    wanted = jnp.max(jnp.where(owned, (remote % blocks)[None, :], 0), axis=1)
+    owned = (block_picks // blocks)[None] == jnp.arange(n, dtype=jnp.int32)[:, None, None]
+    wanted = jnp.max(jnp.where(owned, (block_picks % blocks)[None], 0), axis=(1, 2))
     lanes = -(-n // 128) * 128
     wanted = jnp.pad(wanted, (0, lanes - n)).reshape(1, lanes)
 
@@ -417,7 +414,7 @@
             pltpu.VMEM(keys.shape, jnp.bfloat16),
             pltpu.VMEM(values.shape, jnp.bfloat16),
             pltpu.VMEM((tokens, cols), jnp.bfloat16),
-            pltpu.VMEM((picked * BLOCK_TOKENS, HEAD_SIZE), jnp.bfloat16),
+            pltpu.VMEM((HEAD_SIZE, picked * BLOCK_TOKENS), jnp.bfloat16),
             pltpu.VMEM((picked * BLOCK_TOKENS, 2 * HEAD_SIZE), jnp.bfloat16),
             pltpu.SemaphoreType.DMA((plane - 1,)),
             pltpu.SemaphoreType.DMA((plane - 1,)),
@@ -432,7 +429,7 @@
             pltpu.SemaphoreType.DMA((4,)),
         ],
         compiler_params=pltpu.CompilerParams(
-            collective_id=0, has_side_effects=True, vmem_limit_bytes=48 * 2**20
+            collective_id=0, has_side_effects=True, vmem_limit_bytes=60 * 2**20
         ),
         cost_estimate=pl.CostEstimate(
             flops=4 * tokens * cols * picked * BLOCK_TOKENS,

time: 105 us -> 106 us (level)
    unnamed x7 -> x1, local copies, waits for them, and re-layouts: 4.77 us -> 4.64 us
where the time goes in v4:
time: 106 us
  Pallas kernels  99.7 us (94%)
  local copies, waits for them, and re-layouts  5.16 us (5%)
    pallas_call x1, Pallas kernels, body(): pl.pallas_call(functools.partial(attend_kernel, n, line, parts, groups, b...  99.7 us
    unnamed x1, local copies, waits for them, and re-layouts  4.64 us

profile of v4, /device:TPU:0, one launch (start us, length us, event | category | flops | bytes accessed | tf_op | source)
XLA Modules:
  0.0 105.7 jit_solution(4712003551436212532)
XLA Ops:
  0.0 0.7 add_select_fusion.1
  0.7 0.1 select_reduce_fusion
  0.8 0.5 pad_bitcast_fusion.refs_0_
  1.3 99.7 %shard_map.46 = bf16[256,8192]{1,0:T(8,128)(2,1)} custom-call(s32[1,128]{1,0:T(1,128)} %pad_bitcast_fusion.refs_0_, s32[4,8]{1,0:T(4,128)} %refs_1_.1, bf16[512,4096]{1,0:T(8,128)(2,1)} %refs_2_.1, bf16[4,128,512]{2,1,0:T(8,128)(2,1)} %bitcast.4, bf16[4,128,512]{2,1,0:T(8,128)(2,1)} %bitcast.5), custom_call_target="tpu_custom_call" | custom-call | flops 8589934592 | bytes 8388608 | tf_op jit(solution)/shard_map/pallas_call | solution.py:402
  101.0 4.6 %copy.6 = bf16[256,8192]{1,0:T(8,128)(2,1)} copy(bf16[256,8192]{1,0:T(8,128)(2,1)} %shard_map.46) | data formatting | bytes 8388608

commit v5 on v4

--- a/solution.py
+++ b/solution.py
@@ -50,6 +50,10 @@
     part_chunks = part_rows // chunk
     block_chunks = BLOCK_TOKENS // chunk
     cols = groups * width
+    heads = width // HEAD_SIZE
+    pair = 2 if heads % 2 == 0 else 1
+    pieces = 2 if heads // pair % 2 == 0 else 1
+    piece_cols = width // pieces
 
     k_copy = pltpu.make_async_copy(k_hbm, k_ref, local_sem.at[2])
     v_copy = pltpu.make_async_copy(v_hbm, v_ref, local_sem.at[3])
@@ -178,9 +182,13 @@
                 def _():
                     left_copy(g, k).start()
 
-        if k == 1 and g + 1 < groups:
+        if k == 1 and g <= 1 and g + 1 < groups:
             pack(g + 1)
             begin(g + 1)
+        if k == min(2, last) and g >= 1 and g + 2 < groups:
+            pack(g + 2)
+            begin(g + 2)
+        if k == 1 and g + 1 < groups:
             share(g + 1, owns[g + 1], place)
 
         @pl.when(place >= k)
@@ -215,24 +223,24 @@
     scale = math.log2(math.e) / math.sqrt(HEAD_SIZE)
     first_block = lax.rem(part + 1, parts) * part_rows // BLOCK_TOKENS
 
-    def out_remote(g, index):
+    def out_remote(g, index, piece):
         target = index // part_chunks
         row = pl.multiple_of(lax.rem(index, part_chunks) * chunk, chunk)
-        col = pl.multiple_of(part * cols + g * width, HEAD_SIZE)
+        col = pl.multiple_of(part * cols + g * width + piece * piece_cols, HEAD_SIZE)
         src_row = pl.multiple_of(index * chunk, chunk)
-        src_col = pl.multiple_of(g * width, HEAD_SIZE)
-        src = o_ref.at[pl.ds(src_row, chunk), pl.ds(src_col, width)]
-        dst = out_ref.at[pl.ds(row, chunk), pl.ds(col, width)]
+        src_col = pl.multiple_of(g * width + piece * piece_cols, HEAD_SIZE)
+        src = o_ref.at[pl.ds(src_row, chunk), pl.ds(src_col, piece_cols)]
+        dst = out_ref.at[pl.ds(row, chunk), pl.ds(col, piece_cols)]
         slot = part * part_chunks + lax.rem(index, part_chunks)
         remote = pltpu.make_async_remote_copy(
             src_ref=src,
             dst_ref=dst,
-            send_sem=out_send.at[g, index],
-            recv_sem=out_recv.at[g, slot],
+            send_sem=out_send.at[g, index, piece],
+            recv_sem=out_recv.at[g, slot, piece],
             device_id=(me, target),
             device_id_type=MESH,
         )
-        local = pltpu.make_async_copy(src, dst, out_send.at[g, index])
+        local = pltpu.make_async_copy(src, dst, out_send.at[g, index, piece])
         return target, remote, local
 
     hop_turn = {k: (k - 1) * blocks // (line - 1) + (1 if k > 1 else 0) for k in range(1, line)}
@@ -267,8 +275,6 @@
                     v_sel[rows, :HEAD_SIZE] = chosen[gi][slot, owner // plane, HEAD_SIZE:, :]
 
         q_rows = pl.ds(pl.multiple_of(b * BLOCK_TOKENS, BLOCK_TOKENS), BLOCK_TOKENS)
-        heads = width // HEAD_SIZE
-        pair = 2 if heads % 2 == 0 else 1
         row_id = lax.broadcasted_iota(jnp.int32, (pair * BLOCK_TOKENS, BLOCK_TOKENS), 0)
         key_id = lax.broadcasted_iota(jnp.int32, (pair * BLOCK_TOKENS, BLOCK_TOKENS), 1)
         causal = key_id <= lax.rem(row_id, BLOCK_TOKENS)
@@ -289,6 +295,18 @@
                 own = jnp.where(causal, scores[:, :BLOCK_TOKENS], -jnp.inf)
                 scores = jnp.concatenate([own, scores[:, BLOCK_TOKENS:]], axis=1)
             return scores
+
+        def send_out(piece):
+            for c in range(block_chunks):
+                target, remote, local = out_remote(g, b * block_chunks + c, piece)
+
+                @pl.when(target != part)
+                def _():
+                    remote.start()
+
+                @pl.when(target == part)
+                def _():
+                    local.start()
 
         starts = range(0, span, tile)
         q = load_queries(0)
@@ -310,37 +328,30 @@
             for u in range(pair):
                 o_ref[q_rows, lanes_of(h + u)] = result[u * BLOCK_TOKENS : (u + 1) * BLOCK_TOKENS]
             tiles = following
-        for c in range(block_chunks):
-            target, remote, local = out_remote(g, b * block_chunks + c)
-
-            @pl.when(target != part)
-            def _():
-                remote.start()
-
-            @pl.when(target == part)
-            def _():
-                local.start()
-
+            done = (h + pair) * HEAD_SIZE
+            if done % piece_cols == 0:
+                send_out(done // piece_cols - 1)
         return 0
 
     lax.fori_loop(0, groups * blocks, step, 0)
 
     def finish(t, _):
-        g = t // (parts * part_chunks)
-        index = lax.rem(t, parts * part_chunks)
-        target, remote, local = out_remote(g, index)
+        g = t // (parts * part_chunks * pieces)
+        index = lax.rem(t // pieces, parts * part_chunks)
+        piece = lax.rem(t, pieces)
+        target, remote, local = out_remote(g, index, piece)
 
         @pl.when(target != part)
         def _():
             remote.wait_send()
             row = pl.multiple_of(lax.rem(index, part_chunks) * chunk, chunk)
-            col = pl.multiple_of(target * cols + g * width, HEAD_SIZE)
-            landed = out_ref.at[pl.ds(row, chunk), pl.ds(col, width)]
+            col = pl.multiple_of(target * cols + g * width + piece * piece_cols, HEAD_SIZE)
+            landed = out_ref.at[pl.ds(row, chunk), pl.ds(col, piece_cols)]
             pltpu.make_async_remote_copy(
                 src_ref=landed,
                 dst_ref=landed,
-                send_sem=out_send.at[g, index],
-                recv_sem=out_recv.at[g, index],
+                send_sem=out_send.at[g, index, piece],
+                recv_sem=out_recv.at[g, index, piece],
                 device_id=(me, target),
                 device_id_type=MESH,
             ).wait_recv()
@@ -373,7 +384,7 @@
             def _():
                 left_copy(g, k).wait_send()
 
-    lax.fori_loop(0, groups * parts * part_chunks, finish, 0)
+    lax.fori_loop(0, groups * parts * part_chunks * pieces, finish, 0)
 
 
 def body(line, queries, key_vector_rows, value_vector_rows, block_picks):
@@ -393,6 +404,7 @@
 
     vmem = pl.BlockSpec(memory_space=pltpu.VMEM)
     anywhere = pl.BlockSpec(memory_space=pl.ANY)
+    hbm = pl.BlockSpec(memory_space=pltpu.HBM)
     part_rows = tokens // parts
     chunks = tokens // min(BLOCK_TOKENS, part_rows)
     plane = n // line
@@ -402,7 +414,7 @@
     return pl.pallas_call(
         functools.partial(attend_kernel, n, line, parts, groups, blocks, picked, width),
         out_shape=jax.ShapeDtypeStruct((part_rows, parts * cols), jnp.bfloat16),
-        in_specs=[vmem, pl.BlockSpec(memory_space=pltpu.SMEM), anywhere, anywhere, anywhere],
+        in_specs=[vmem, pl.BlockSpec(memory_space=pltpu.SMEM), hbm, hbm, hbm],
         out_specs=anywhere,
         scratch_shapes=[shard] * (groups * (2 * line - 1))
         + [stage] * groups
@@ -424,12 +436,12 @@
             pltpu.SemaphoreType.DMA((groups, line)),
             pltpu.SemaphoreType.DMA((groups, plane - 1, line)),
             pltpu.SemaphoreType.DMA((groups, plane - 1, line)),
-            pltpu.SemaphoreType.DMA((groups, chunks)),
-            pltpu.SemaphoreType.DMA((groups, chunks)),
+            pltpu.SemaphoreType.DMA((groups, chunks, 2)),
+            pltpu.SemaphoreType.DMA((groups, chunks, 2)),
             pltpu.SemaphoreType.DMA((4,)),
         ],
         compiler_params=pltpu.CompilerParams(
-            collective_id=0, has_side_effects=True, vmem_limit_bytes=60 * 2**20
+            collective_id=0, has_side_effects=True, vmem_limit_bytes=48 * 2**20
         ),
         cost_estimate=pl.CostEstimate(
             flops=4 * tokens * cols * picked * BLOCK_TOKENS,

time: 106 us -> 106 us (level)
    unnamed x1 -> x7, local copies, waits for them, and re-layouts: 4.64 us -> 4.77 us
where the time goes in v5:
time: 106 us
  Pallas kernels  100 us (94%)
  local copies, waits for them, and re-layouts  4.78 us (5%)
    pallas_call x1, Pallas kernels, body(): pl.pallas_call(functools.partial(attend_kernel, n, line, parts, groups, b...  100 us
    unnamed x7, local copies, waits for them, and re-layouts  4.77 us

profile of v5, /device:TPU:0, one launch (start us, length us, event | category | flops | bytes accessed | tf_op | source)
XLA Modules:
  0.0 105.8 jit_solution(17896141781491355283)
XLA Ops:
  0.0 0.7 add_select_fusion.1
  0.7 0.1 select_reduce_fusion
  0.8 0.0 copy-start
  0.8 0.7 copy-done
  1.5 0.0 copy-start.1
  1.5 1.0 copy-done.1
  2.5 0.0 copy-start.2
  2.5 1.0 copy-done.2
  3.6 100.2 %shard_map.46 = bf16[256,8192]{1,0:T(8,128)(2,1)S(1)} custom-call(s32[1,128]{1,0:T(1,128)S(1)} %pad_bitcast_fusion.refs_0_, s32[4,8]{1,0:T(4,128)S(1)} %copy-done, bf16[512,4096]{1,0:T(8,128)(2,1)} %refs_2_.1, bf16[4,128,512]{2,1,0:T(8,128)(2,1)S(1)} %bitcast.4, bf16[4,128,512]{2,1,0:T(8,128)(2,1)S(1)} %bitcast.5), custom_call_target="tpu_custom_call" | custom-call | flops 8589934592 | bytes 8388608 | tf_op jit(solution)/shard_map/pallas_call | solution.py:414
  103.8 2.0 %copy.6 = bf16[256,8192]{1,0:T(8,128)(2,1)} copy(bf16[256,8192]{1,0:T(8,128)(2,1)S(1)} %shard_map.46) | data formatting | bytes 8388608
  (1 shorter events, 0.0 us)
Async XLA Ops:
  0.8 0.7 copy-start
  1.5 1.0 copy-start.1
  2.5 1.0 copy-start.2

commit v6 on v5

--- a/solution.py
+++ b/solution.py
@@ -111,22 +111,22 @@
             device_id_type=MESH,
         )
 
-    def right_copy(g, k):
+    def right_copy(g, k, i):
         return pltpu.make_async_remote_copy(
-            src_ref=owns[g] if k == 0 else from_left[g * (line - 1) + k - 1],
-            dst_ref=from_left[g * (line - 1) + k],
-            send_sem=right_send.at[g, k],
-            recv_sem=left_recv.at[g, k],
+            src_ref=(owns[g] if k == 0 else from_left[g * (line - 1) + k - 1]).at[i],
+            dst_ref=from_left[g * (line - 1) + k].at[i],
+            send_sem=right_send.at[g, k, i],
+            recv_sem=left_recv.at[g, k, i],
             device_id=(me + plane, part),
             device_id_type=MESH,
         )
 
-    def left_copy(g, k):
+    def left_copy(g, k, i):
         return pltpu.make_async_remote_copy(
-            src_ref=owns[g] if k == 0 else from_right[g * (line - 1) + k - 1],
-            dst_ref=from_right[g * (line - 1) + k],
-            send_sem=left_send.at[g, k],
-            recv_sem=right_recv.at[g, k],
+            src_ref=(owns[g] if k == 0 else from_right[g * (line - 1) + k - 1]).at[i],
+            dst_ref=from_right[g * (line - 1) + k].at[i],
+            send_sem=left_send.at[g, k, i],
+            recv_sem=right_recv.at[g, k, i],
             device_id=(me - plane, part),
             device_id_type=MESH,
         )
@@ -155,32 +155,36 @@
     def begin(g):
         @pl.when(place < line - 1)
         def _():
-            right_copy(g, 0).start()
+            for i in range(blocks):
+                right_copy(g, 0, i).start()
 
         @pl.when(place > 0)
         def _():
-            left_copy(g, 0).start()
+            for i in range(blocks):
+                left_copy(g, 0, i).start()
 
     def hop(g, k):
         last = line - 1
 
         @pl.when(place >= k)
         def _():
-            right_copy(g, k - 1).wait_recv()
-            if k < last:
-
-                @pl.when(place < last)
-                def _():
-                    right_copy(g, k).start()
+            for i in range(blocks):
+                right_copy(g, k - 1, i).wait_recv()
+                if k < last:
+
+                    @pl.when(place < last)
+                    def _():
+                        right_copy(g, k, i).start()
 
         @pl.when(place + k <= last)
         def _():
-            left_copy(g, k - 1).wait_recv()
-            if k < last:
-
-                @pl.when(place > 0)
-                def _():
-                    left_copy(g, k).start()
+            for i in range(blocks):
+                left_copy(g, k - 1, i).wait_recv()
+                if k < last:
+
+                    @pl.when(place > 0)
+                    def _():
+                        left_copy(g, k, i).start()
 
         if k == 1 and g <= 1 and g + 1 < groups:
             pack(g + 1)
@@ -378,11 +382,13 @@
 
             @pl.when(jnp.logical_and(place < line - 1, place >= k))
             def _():
-                right_copy(g, k).wait_send()
+                for i in range(blocks):
+                    right_copy(g, k, i).wait_send()
 
             @pl.when(jnp.logical_and(place > 0, place + k <= line - 1))
             def _():
-                left_copy(g, k).wait_send()
+                for i in range(blocks):
+                    left_copy(g, k, i).wait_send()
 
     lax.fori_loop(0, groups * parts * part_chunks * pieces, finish, 0)
 
@@ -430,10 +436,10 @@
             pltpu.VMEM((picked * BLOCK_TOKENS, 2 * HEAD_SIZE), jnp.bfloat16),
             pltpu.SemaphoreType.DMA((plane - 1,)),
             pltpu.SemaphoreType.DMA((plane - 1,)),
-            pltpu.SemaphoreType.DMA((groups, line)),
-            pltpu.SemaphoreType.DMA((groups, line)),
-            pltpu.SemaphoreType.DMA((groups, line)),
-            pltpu.SemaphoreType.DMA((groups, line)),
+            pltpu.SemaphoreType.DMA((groups, line, blocks)),
+            pltpu.SemaphoreType.DMA((groups, line, blocks)),
+            pltpu.SemaphoreType.DMA((groups, line, blocks)),
+            pltpu.SemaphoreType.DMA((groups, line, blocks)),
             pltpu.SemaphoreType.DMA((groups, plane - 1, line)),
             pltpu.SemaphoreType.DMA((groups, plane - 1, line)),
             pltpu.SemaphoreType.DMA((groups, chunks, 2)),

time: 106 us -> 108 us (1.019)
  Pallas kernels: 100 us -> 102 us
    pallas_call x1, Pallas kernels: 100 us -> 102 us  [body(): pl.pallas_call(functools.partial(attend_kernel, n, line, parts, groups, b...]
where the time goes in v6:
time: 108 us
  Pallas kernels  102 us (94%)
  local copies, waits for them, and re-layouts  4.78 us (4%)
    pallas_call x1, Pallas kernels, body(): pl.pallas_call(functools.partial(attend_kernel, n, line, parts, groups, b...  102 us
    unnamed x7, local copies, waits for them, and re-layouts  4.77 us

profile of v6, /device:TPU:0, one launch (start us, length us, event | category | flops | bytes accessed | tf_op | source)
XLA Modules:
  0.0 107.7 jit_solution(8106492696091035976)
XLA Ops:
  0.0 0.7 add_select_fusion.1
  0.7 0.1 select_reduce_fusion
  0.8 0.0 copy-start
  0.8 0.7 copy-done
  1.5 0.0 copy-start.1
  1.5 1.0 copy-done.1
  2.5 0.0 copy-start.2
  2.5 1.0 copy-done.2
  3.6 102.1 %shard_map.46 = bf16[256,8192]{1,0:T(8,128)(2,1)S(1)} custom-call(s32[1,128]{1,0:T(1,128)S(1)} %pad_bitcast_fusion.refs_0_, s32[4,8]{1,0:T(4,128)S(1)} %copy-done, bf16[512,4096]{1,0:T(8,128)(2,1)} %refs_2_.1, bf16[4,128,512]{2,1,0:T(8,128)(2,1)S(1)} %bitcast.4, bf16[4,128,512]{2,1,0:T(8,128)(2,1)S(1)} %bitcast.5), custom_call_target="tpu_custom_call" | custom-call | flops 8589934592 | bytes 8388608 | tf_op jit(solution)/shard_map/pallas_call | solution.py:420
  105.7 2.0 %copy.6 = bf16[256,8192]{1,0:T(8,128)(2,1)} copy(bf16[256,8192]{1,0:T(8,128)(2,1)S(1)} %shard_map.46) | data formatting | bytes 8388608
  (1 shorter events, 0.0 us)
Async XLA Ops:
  0.8 0.7 copy-start
  1.5 1.0 copy-start.1
  2.5 1.0 copy-start.2
